TPU v7x, 128 devices: a whole 4x4x4 slice. The times are simulated.
128 devices in a mesh: row: 8 (over y_lo, x), col: 16 (over z, y_hi, core).
Axes of the slice: x: 4, y: 4 (y_hi: 2, y_lo: 2; y = y_hi * 2 + y_lo), z: 4, core: 2. Of those that a mesh axis runs over, the one named last changes fastest.
Arguments:
- hidden_in: bfloat16 [2048, 8192], P('col', 'row'), may hold values from -130 to 130
- norm_gain: float32 [8192], P('row'), may hold values from 0.5 to 1.5
- w_query: bfloat16 [8192, 8192], P('row', 'col'), may hold values from -0.0625 to 0.0625
- scale_query: float32 [64, 64], P('row', 'col'), may hold values from 0.35 to 2.8
- bias_query: float32 [8192], P('col'), may hold values from -14 to 14
- w_keyval: bfloat16 [8192, 2048], P('row'), may hold values from -0.0625 to 0.0625
- scale_keyval: float32 [64, 16], P('row'), may hold values from 0.35 to 2.8
- bias_keyval: float32 [2048], replicated, may hold values from -3 to 3
- w_out: bfloat16 [8192, 8192], P('col', 'row'), may hold values from -0.0625 to 0.0625
- scale_out: float32 [64, 64], P('col', 'row'), may hold values from 0.35 to 2.8
- cache_keyval: bfloat16 [2, 8192, 1024], P(None, 'row'), may hold values from -14 to 14
- span_offset: int32 [1], replicated, may hold values from 2048 to 8192
Outputs:
- hidden_out: bfloat16 [2048, 8192], P('col', 'row')
All inputs are finite; a program needn't handle non-finite values.
Results may differ from a plain program's by a relative error of at most 0.033.
Values may be sent and summed in bfloat16 or wider, within the bound.
No kernel may reach another device: no remote copies, remote signals or barrier semaphores. Data moves between devices by JAX's collectives and lax.ppermute only.
A program may use at most 192 MiB of HBM per device.

v0:
```python
import math
import jax
import jax.numpy as jnp
from jax import lax
from jax.sharding import PartitionSpec as P

D = 8192
H = 64
KVH = 8
HD = 128
QB = 128
EPSILON = 1e-06
ROPE_BASE = 1000000.0
MASKED = -1e30


def dequantize(weight, block_scale):
    expanded = jnp.repeat(jnp.repeat(block_scale, QB, axis=0), QB, axis=1)
    return (weight.astype(jnp.float32) * expanded).astype(jnp.bfloat16)


def rotate(vectors, positions):
    half_dim = HD // 2
    inverse = ROPE_BASE ** (-(2.0 * jnp.arange(half_dim, dtype=jnp.float32)) / HD)
    angles = positions[:, None] * inverse[None, :]
    cosine = jnp.cos(angles)[:, None, :]
    sine_part = jnp.sin(angles)[:, None, :]
    first_half = vectors[..., :half_dim]
    second = vectors[..., half_dim:]
    return jnp.concatenate(
        [first_half * cosine - second * sine_part, second * cosine + first_half * sine_part],
        axis=-1,
    )


def block_scores(queries, key_block, key_index, query_index, offset, cache_len):
    scores = jnp.einsum("thd,kd->htk", queries, key_block, preferred_element_type=jnp.float32) * (
        1.0 / math.sqrt(HD)
    )
    earlier = (key_index < cache_len)[None, :]
    allowed = jnp.where(
        earlier,
        (key_index < offset)[None, :],
        (key_index - cache_len)[None, :] <= query_index[:, None],
    )
    return jnp.where(allowed[None, :, :], scores, MASKED)


def score_blocks(queries, key_rows, key_index, query_index, offset, cache_len, block_len):
    key_blocks = key_rows.reshape(-1, block_len, key_rows.shape[-1])
    index_blocks = key_index.reshape(-1, block_len)

    def one_block(block_item):
        return block_scores(queries, block_item[0], block_item[1], query_index, offset, cache_len)

    return lax.map(one_block, (key_blocks, index_blocks))


def block_stats(scores):
    row_peak = jnp.max(scores, axis=(0, 3))
    weights = jnp.where(scores > 0.5 * MASKED, jnp.exp(scores - row_peak[None, :, :, None]), 0.0)
    return (row_peak, jnp.sum(weights, axis=(0, 3)))


def weighted_values(scores, value_rows, block_len, row_peak, row_total):
    value_blocks = value_rows.reshape(-1, block_len, value_rows.shape[-1])

    def advance(summed, block_item):
        weights = (jnp.exp(block_item[0] - row_peak[:, :, None]) / row_total[:, :, None]).astype(
            jnp.bfloat16
        )
        return (
            summed
            + jnp.einsum("htk,kd->thd", weights, block_item[1], preferred_element_type=jnp.float32),
            None,
        )

    start_state = jnp.zeros((scores.shape[2], scores.shape[1], HD), jnp.float32)
    return lax.scan(advance, start_state, (scores, value_blocks))[0]


def body(
    hidden_in,
    norm_gain,
    w_query,
    scale_query,
    bias_query,
    w_keyval,
    scale_keyval,
    bias_keyval,
    w_out,
    scale_out,
    cache_keyval,
    span_offset,
):
    row_count = lax.axis_size("row")
    row_index = lax.axis_index("row")
    col_index = lax.axis_index("col")
    widened = hidden_in.astype(jnp.float32)
    squares = lax.psum(jnp.sum(widened * widened, axis=1), "row")
    norm_ratio = lax.rsqrt(squares / D + EPSILON)
    normed = (widened * norm_ratio[:, None] * norm_gain[None, :]).astype(jnp.bfloat16)
    gathered = lax.all_gather(normed, "col", axis=0, tiled=True)
    tokens = gathered.shape[0]
    tok_dev = tokens // row_count
    heads_dev = w_query.shape[1] // HD
    qwidth = heads_dev * HD
    group_size = H // KVH
    kv_width = KVH * HD
    kv_head = col_index * heads_dev // group_size
    key_cols = lax.dynamic_slice_in_dim(w_keyval, kv_head * HD, HD, 1)
    value_cols = lax.dynamic_slice_in_dim(w_keyval, kv_width + kv_head * HD, HD, 1)
    key_scale = lax.dynamic_slice_in_dim(scale_keyval, kv_head * (HD // QB), HD // QB, 1)
    value_scale = lax.dynamic_slice_in_dim(
        scale_keyval, (kv_width + kv_head * HD) // QB, HD // QB, 1
    )
    combined = jnp.concatenate(
        [
            dequantize(w_query, scale_query),
            dequantize(key_cols, key_scale),
            dequantize(value_cols, value_scale),
        ],
        axis=1,
    )
    projected = lax.psum_scatter(
        jnp.dot(gathered, combined, preferred_element_type=jnp.float32).astype(jnp.bfloat16),
        "row",
        scatter_dimension=0,
        tiled=True,
    ).astype(jnp.float32)
    bias_key = lax.dynamic_slice_in_dim(bias_keyval, kv_head * HD, HD, 0)
    bias_value = lax.dynamic_slice_in_dim(bias_keyval, kv_width + kv_head * HD, HD, 0)
    offset = span_offset[0]
    query_index = row_index * tok_dev + jnp.arange(tok_dev, dtype=jnp.int32)
    positions = (offset + query_index).astype(jnp.float32)
    queries = rotate(
        (projected[:, :qwidth] + bias_query[None, :]).reshape(tok_dev, heads_dev, HD), positions
    ).astype(jnp.bfloat16)
    own_keys = rotate(
        (projected[:, qwidth : qwidth + HD] + bias_key[None, :]).reshape(tok_dev, 1, HD), positions
    )
    own_keys = own_keys.reshape(tok_dev, HD).astype(jnp.bfloat16)
    own_values = (projected[:, qwidth + HD :] + bias_value[None, :]).astype(jnp.bfloat16)
    span_kv = lax.all_gather(
        jnp.concatenate([own_keys, own_values], axis=1), "row", axis=0, tiled=True
    )
    span_keys = span_kv[:, :HD]
    span_values = span_kv[:, HD:]
    cache_dev = cache_keyval.shape[1]
    cache_len = cache_dev * row_count
    cache_head = lax.dynamic_slice_in_dim(cache_keyval, kv_head * HD, HD, 2)
    span_index = cache_len + jnp.arange(tokens, dtype=jnp.int32)
    all_queries = lax.all_gather(
        queries.reshape(tok_dev, qwidth), "row", axis=0, tiled=True
    ).reshape(tokens, heads_dev, HD)
    every_index = jnp.arange(tokens, dtype=jnp.int32)
    cache_index = row_index * cache_dev + jnp.arange(cache_dev, dtype=jnp.int32)
    cache_scores = score_blocks(
        all_queries, cache_head[0], cache_index, every_index, offset, cache_len, tok_dev
    )
    cache_peak, cache_total = block_stats(cache_scores)
    own_scores = score_blocks(
        queries, span_keys, span_index, query_index, offset, cache_len, tokens
    )
    own_peak, own_total = block_stats(own_scores)
    first_row = row_index * tok_dev
    placed_peak = lax.dynamic_update_slice_in_dim(
        jnp.full_like(cache_peak, MASKED), own_peak, first_row, 1
    )
    peak_all = lax.pmax(jnp.maximum(cache_peak, placed_peak).astype(jnp.bfloat16), "row").astype(
        jnp.float32
    )
    peak_own = lax.dynamic_slice_in_dim(peak_all, first_row, tok_dev, 1)
    placed_total = lax.dynamic_update_slice_in_dim(
        jnp.zeros_like(cache_total), own_total * jnp.exp(own_peak - peak_own), first_row, 1
    )
    total_all = lax.psum(
        (cache_total * jnp.exp(cache_peak - peak_all) + placed_total).astype(jnp.bfloat16), "row"
    ).astype(jnp.float32)
    total_own = lax.dynamic_slice_in_dim(total_all, first_row, tok_dev, 1)
    cache_part = weighted_values(cache_scores, cache_head[1], tok_dev, peak_all, total_all)
    cache_share = lax.psum_scatter(
        cache_part.reshape(tokens, qwidth).astype(jnp.bfloat16),
        "row",
        scatter_dimension=0,
        tiled=True,
    ).astype(jnp.float32)
    span_part = weighted_values(own_scores, span_values, tokens, peak_own, total_own)
    attended = cache_share.reshape(tok_dev, heads_dev, HD) + span_part
    attended = attended.reshape(tok_dev, qwidth).astype(jnp.bfloat16)
    attention_all = lax.all_gather(attended, "row", axis=0, tiled=True)
    out_weight = dequantize(w_out, scale_out)
    mixed_out = lax.psum_scatter(
        jnp.dot(attention_all, out_weight, preferred_element_type=jnp.float32).astype(jnp.bfloat16),
        "col",
        scatter_dimension=0,
        tiled=True,
    )
    return mixed_out


def solution(mesh):
    return jax.shard_map(
        body,
        mesh=mesh,
        in_specs=(
            P("col", "row"),
            P("row"),
            P("row", "col"),
            P("row", "col"),
            P("col"),
            P("row", None),
            P("row", None),
            P(),
            P("col", "row"),
            P("col", "row"),
            P(None, "row", None),
            P(),
        ),
        out_specs=P("col", "row"),
        check_vma=False,
    )
```

profile of v0, /device:TPU:0, one launch (start us, length us, event | category | flops | bytes accessed | tf_op | source)
XLA Modules:
  0.0 627.0 jit_solution(3063638257543192442)
XLA Ops:
  7.7 19.8 %psum.14 = f32[128]{0:T(128)S(1)} all-reduce(f32[128]{0:T(128)S(1)} %fusion.27), channel_id=1, replica_groups=mesh['row'=8,'col'=16] {'row'}, use_global_device_ids=true, to_apply=%region_1.0 | all-reduce | flops 128 | bytes 1024 | tf_op jit(solution)/shard_map/psum | solution.py:100
  34.3 50.2 %all-gather.5.cloned.1.call-done = bf16[2048,1024]{1,0:T(8,128)(2,1)} async-done(((bf16[128,1024]{1,0:T(8,128)(2,1)}), bf16[2048,1024]{1,0:T(8,128)(2,1)}) %all-gather.5.cloned.1.call-update) | async-done | bytes 4194320 | tf_op jit(solution)/shard_map/all_gather | solution.py:103
  93.3 42.3 %reduce-scatter.4.cloned.1.call-done = bf16[256,768]{0,1:T(8,128)(2,1)} async-done(((bf16[2048,768]{0,1:T(8,128)(2,1)}), bf16[256,768]{0,1:T(8,128)(2,1)}) %reduce-scatter.4.cloned.1.call-update) | async-done | bytes 393232 | tf_op jit(solution)/shard_map/reduce_scatter | solution.py:125
  143.1 31.9 %all-gather.9.cloned.1.call-done = bf16[2048,256]{0,1:T(8,128)(2,1)} async-done(((bf16[256,256]{0,1:T(8,128)(2,1)}), bf16[2048,256]{0,1:T(8,128)(2,1)}) %all-gather.9.cloned.1.call-update) | async-done | bytes 1048592 | tf_op jit(solution)/shard_map/all_gather | solution.py:144
  183.1 40.4 %all-gather.7.cloned.1.call-done = bf16[2048,512]{0,1:T(8,128)(2,1)} async-done(((bf16[256,512]{0,1:T(8,128)(2,1)}), bf16[2048,512]{0,1:T(8,128)(2,1)}) %all-gather.7.cloned.1.call-update) | async-done | bytes 2097168 | tf_op jit(solution)/shard_map/all_gather | solution.py:153
  226.6 24.4 %while.34 = (s32[]{:T(128)}, f32[4,4,2048,256]{2,3,1,0:T(8,128)}, s32[4,256]{1,0:T(4,128)S(1)}, s32[]{:T(128)}, bf16[4,256,128]{2,1,0:T(8,128)(2,1)S(1)}, /*index=5*/bf16[2048,4,128]{2,0,1:T(8,128)(2,1)S(1)}) while((s32[]{:T(128)}, f32[4,4,2048,256]{2,3,1,0:T(8,128)}, s32[4,256]{1,0:T(4,128)S(1)}, s32[]{:T(128)}, ...), condition=%wide.region_4.5_spmd.clone.clone, body=%wide.region_3.4_spmd.clone.sunk.clone | while | flops 542114560 | bytes 11606097 | solution.py:56
  250.9 12.0 %reduce_max.18 = f32[4,2048]{1,0:T(4,128)S(1)} reduce(f32[4,4,2048,256]{2,3,1,0:T(8,128)} %get-tuple-element.414, f32[]{:T(128)} %constant.145.clone.1), dimensions={0,3}, to_apply=%region_5.6 | reduce | flops 8380416 | bytes 33587204 | tf_op jit(solution)/shard_map/reduce_max | solution.py:60
  262.9 14.1 %select_reduce_fusion = f32[4,2048]{1,0:T(4,128)S(1)} fusion(f32[4,4,2048,256]{2,3,1,0:T(8,128)} %get-tuple-element.414, f32[4,2048]{1,0:T(4,128)S(1)} %reduce_max.18), kind=kLoop, calls=%fused_computation.20 | loop fusion | flops 33546240 | bytes 33619968 | tf_op jit(solution)/shard_map/reduce_sum | solution.py:62
  277.0 33.2 %pmax.7 = bf16[4,2048]{1,0:T(4,128)(2,1)S(1)} all-reduce(bf16[4,2048]{1,0:T(4,128)(2,1)S(1)} %max.7), channel_id=1, replica_groups=mesh['row'=8,'col'=16] {'row'}, use_global_device_ids=true, to_apply=%region_7.8 | all-reduce | flops 8192 | bytes 32768 | tf_op jit(solution)/shard_map/pmax | solution.py:170
  310.3 30.6 %psum.15 = bf16[4,2048]{1,0:T(4,128)(2,1)S(1)} all-reduce(bf16[4,2048]{1,0:T(4,128)(2,1)S(1)} %convert_element_type.113), channel_id=1, replica_groups=mesh['row'=8,'col'=16] {'row'}, use_global_device_ids=true, to_apply=%region_10.11 | all-reduce | flops 8192 | bytes 32768 | tf_op jit(solution)/shard_map/psum | solution.py:177
  340.9 95.2 %while.35 = (s32[]{:T(128)}, f32[2048,4,128]{0,2,1:T(8,128)}, bf16[4,256,128]{2,1,0:T(8,128)(2,1)S(1)}, f32[4,4,2048,256]{2,3,1,0:T(8,128)}, f32[4,2048]{1,0:T(4,128)S(1)}, /*index=5*/f32[4,2048]{1,0:T(4,128)S(1)}) while((s32[]{:T(128)}, f32[2048,4,128]{0,2,1:T(8,128)}, bf16[4,256,128]{2,1,0:T(8,128)(2,1)S(1)}, ...), condition=%wide.region_12.13_spmd.clone.clone, body=%wide.region_11.12_spmd.clone.sunk.clone | while | flops 545259520 | bytes 50462804 | solution.py:79
  340.9 7.7 %constant_dynamic-slice_fusion.8 = f32[1,4,2048,256]{2,3,1,0:T(8,128)} fusion(f32[4,4,2048,256]{2,3,1,0:T(8,128)} %get-tuple-element.426, s32[]{:T(128)} %get-tuple-element.417), kind=kLoop, calls=%fused_computation.7.clone.1.clone | loop fusion | bytes 16777220 | tf_op jit(solution)/shard_map/while/body/jit(dynamic_index_in_dim)/dynamic_slice | solution.py:79
  348.6 8.7 %copy.53 = f32[1,4,2048,256]{3,2,1,0:T(8,128)} copy(f32[1,4,2048,256]{2,3,1,0:T(8,128)} %constant_dynamic-slice_fusion.8) | data formatting | bytes 16777216 | tf_op jit(solution)/shard_map/while/body/jit(dynamic_index_in_dim)/dynamic_slice | solution.py:79
  364.1 7.7 %constant_dynamic-slice_fusion.8 = f32[1,4,2048,256]{2,3,1,0:T(8,128)} fusion(f32[4,4,2048,256]{2,3,1,0:T(8,128)} %get-tuple-element.426, s32[]{:T(128)} %get-tuple-element.417), kind=kLoop, calls=%fused_computation.7.clone.1.clone | loop fusion | bytes 16777220 | tf_op jit(solution)/shard_map/while/body/jit(dynamic_index_in_dim)/dynamic_slice | solution.py:79
  371.8 8.7 %copy.53 = f32[1,4,2048,256]{3,2,1,0:T(8,128)} copy(f32[1,4,2048,256]{2,3,1,0:T(8,128)} %constant_dynamic-slice_fusion.8) | data formatting | bytes 16777216 | tf_op jit(solution)/shard_map/while/body/jit(dynamic_index_in_dim)/dynamic_slice | solution.py:79
  388.1 7.7 %constant_dynamic-slice_fusion.8 = f32[1,4,2048,256]{2,3,1,0:T(8,128)} fusion(f32[4,4,2048,256]{2,3,1,0:T(8,128)} %get-tuple-element.426, s32[]{:T(128)} %get-tuple-element.417), kind=kLoop, calls=%fused_computation.7.clone.1.clone | loop fusion | bytes 16777220 | tf_op jit(solution)/shard_map/while/body/jit(dynamic_index_in_dim)/dynamic_slice | solution.py:79
  395.8 8.7 %copy.53 = f32[1,4,2048,256]{3,2,1,0:T(8,128)} copy(f32[1,4,2048,256]{2,3,1,0:T(8,128)} %constant_dynamic-slice_fusion.8) | data formatting | bytes 16777216 | tf_op jit(solution)/shard_map/while/body/jit(dynamic_index_in_dim)/dynamic_slice | solution.py:79
  404.5 7.6 %bitcast_add_fusion.3 = f32[2048,4,128]{0,2,1:T(8,128)} fusion(f32[2048,4,128]{0,2,1:T(8,128)} %get-tuple-element.418, f32[4,2048]{1,0:T(4,128)S(1)} %get-tuple-element.428, f32[1,4,2048,256]{3,2,1,0:T(8,128)} %copy.53, f32[4,2048]{1,0:T(4,128)S(1)} %get-tuple-element.427, pred[]{:T(512)S(6)} %compare.8, ...), kind=kOutput, calls=%fused_computation.2.clone.1.clone | convolution fusion | flops 545259520 | bytes 16908292 | tf_op jit(solution)/shard_map/while/body/eval_jaxpr/htk,kd->thd/dot_general | solution.py:74
  412.2 7.7 %constant_dynamic-slice_fusion.8 = f32[1,4,2048,256]{2,3,1,0:T(8,128)} fusion(f32[4,4,2048,256]{2,3,1,0:T(8,128)} %get-tuple-element.426, s32[]{:T(128)} %get-tuple-element.417), kind=kLoop, calls=%fused_computation.7.clone.1.clone | loop fusion | bytes 16777220 | tf_op jit(solution)/shard_map/while/body/jit(dynamic_index_in_dim)/dynamic_slice | solution.py:79
  419.8 8.7 %copy.53 = f32[1,4,2048,256]{3,2,1,0:T(8,128)} copy(f32[1,4,2048,256]{2,3,1,0:T(8,128)} %constant_dynamic-slice_fusion.8) | data formatting | bytes 16777216 | tf_op jit(solution)/shard_map/while/body/jit(dynamic_index_in_dim)/dynamic_slice | solution.py:79
  428.5 7.6 %bitcast_add_fusion.3 = f32[2048,4,128]{0,2,1:T(8,128)} fusion(f32[2048,4,128]{0,2,1:T(8,128)} %get-tuple-element.418, f32[4,2048]{1,0:T(4,128)S(1)} %get-tuple-element.428, f32[1,4,2048,256]{3,2,1,0:T(8,128)} %copy.53, f32[4,2048]{1,0:T(4,128)S(1)} %get-tuple-element.427, pred[]{:T(512)S(6)} %compare.8, ...), kind=kOutput, calls=%fused_computation.2.clone.1.clone | convolution fusion | flops 545259520 | bytes 16908292 | tf_op jit(solution)/shard_map/while/body/eval_jaxpr/htk,kd->thd/dot_general | solution.py:74
  440.2 41.3 %reduce-scatter.6.cloned.1.call-done = bf16[256,512]{0,1:T(8,128)(2,1)} async-done(((bf16[2048,512]{0,1:T(8,128)(2,1)}), bf16[256,512]{0,1:T(8,128)(2,1)}) %reduce-scatter.6.cloned.1.call-update) | async-done | bytes 262160 | tf_op jit(solution)/shard_map/reduce_scatter | solution.py:182
  487.6 44.1 %all-gather.11.cloned.1.call-done = bf16[2048,512]{0,1:T(8,128)(2,1)} async-done(((bf16[256,512]{0,1:T(8,128)(2,1)}), bf16[2048,512]{0,1:T(8,128)(2,1)}) %all-gather.11.cloned.1.call-update) | async-done | bytes 2097168 | tf_op jit(solution)/shard_map/all_gather | solution.py:191
  538.3 81.9 %reduce-scatter.8.cloned.1.call-done = bf16[128,1024]{1,0:T(8,128)(2,1)} async-done(((bf16[2048,1024]{1,0:T(8,128)(2,1)}), bf16[128,1024]{1,0:T(8,128)(2,1)}) %reduce-scatter.8.cloned.1.call-update) | async-done | bytes 262160 | tf_op jit(solution)/shard_map/reduce_scatter | solution.py:193
  (95 shorter events, 89.8 us)
Async XLA Ops:
  6.5 27.4 %copy-start.1 = (bf16[1024,512]{1,0:T(8,128)(2,1)S(1)}, bf16[1024,512]{1,0:T(8,128)(2,1)}, u32[]{:S(2)}) copy-start(bf16[1024,512]{1,0:T(8,128)(2,1)} %param.18) | copy-start | bytes 3145732
  6.5 78.0 %all-gather.5.cloned.1.call-start = ((), (), s32[]{:S(2)}) async-start(), calls=%async_computation.3 | async-start | bytes 4456448 | tf_op jit(solution)/shard_map/all_gather | solution.py:103
  29.3 106.3 %reduce-scatter.4.cloned.1.call-start = ((), (), s32[]{:S(2)}) async-start(), calls=%async_computation.4 | async-start | bytes 3538944 | tf_op jit(solution)/shard_map/reduce_scatter | solution.py:125
  91.8 46.6 %copy-start.3 = (f32[512]{0:T(512)S(1)}, f32[512]{0:T(512)}, u32[]{:S(2)}) copy-start(f32[512]{0:T(512)} %param.20) | copy-start | bytes 6148
  91.8 83.2 %all-gather.9.cloned.1.call-start = ((), (), s32[]{:S(2)}) async-start(), calls=%async_computation.6 | async-start | bytes 1179648 | tf_op jit(solution)/shard_map/all_gather | solution.py:144
  137.9 85.7 %all-gather.7.cloned.1.call-start = ((), (), s32[]{:S(2)}) async-start(), calls=%async_computation.5 | async-start | bytes 2359296 | tf_op jit(solution)/shard_map/all_gather | solution.py:153
  140.2 341.3 %reduce-scatter.6.cloned.1.call-start = ((), (), s32[]{:S(2)}) async-start(), calls=%async_computation.7 | async-start | bytes 2359296 | tf_op jit(solution)/shard_map/reduce_scatter | solution.py:182
  177.6 3.2 copy-start
  436.2 45.4 %copy-start.2 = (bf16[2048,256]{0,1:T(8,128)(2,1)S(1)}, bf16[2048,256]{0,1:T(8,128)(2,1)}, u32[]{:S(2)}) copy-start(bf16[2048,256]{0,1:T(8,128)(2,1)} %all-gather.9.cloned.1.call-done) | copy-start | bytes 3145732
  440.1 91.5 %all-gather.11.cloned.1.call-start = ((), (), s32[]{:S(2)}) async-start(), calls=%async_computation.8 | async-start | bytes 2359296 | tf_op jit(solution)/shard_map/all_gather | solution.py:191
  481.6 50.1 %copy-start.4 = (f32[4,8]{1,0:T(4,128)S(1)}, f32[4,8]{1,0:T(4,128)}, u32[]{:S(2)}) copy-start(f32[4,8]{1,0:T(4,128)} %param.25) | copy-start | bytes 388
  481.6 50.7 %copy-start.5 = (bf16[512,1024]{1,0:T(8,128)(2,1)S(1)}, bf16[512,1024]{1,0:T(8,128)(2,1)}, u32[]{:S(2)}) copy-start(bf16[512,1024]{1,0:T(8,128)(2,1)} %param.24) | copy-start | bytes 3145732
  487.3 132.9 %reduce-scatter.8.cloned.1.call-start = ((), (), s32[]{:S(2)}) async-start(), calls=%async_computation.9 | async-start | bytes 4456448 | tf_op jit(solution)/shard_map/reduce_scatter | solution.py:193
Sparse Core Ops, SparseCore 0:
  29.5 55.0 all-gather.4
  91.9 43.6 reduce-scatter.3
  138.0 36.9 all-gather.8
  176.4 47.0 all-gather.6
  440.3 41.2 reduce-scatter.5
  487.4 44.1 all-gather.10
  538.4 81.7 reduce-scatter.7
where the time goes:
time: 628 us; the launch traced here: 627 us
  waiting for transfers between devices  332 us (53%)
  blocking collectives  83.6 us (13%)
  local copies, waits for them, and re-layouts  78.6 us (13%)
  matrix products  70.3 us (11%)
  other arithmetic  47 us (7%)
  between operations  14.4 us (2%)
    reduce_scatter x1, waiting for transfers between devices, body(): lax.psum_scatter(jnp.dot(attention_all, out_weight, preferred_element_typ...  81.9 us
    dynamic_slice x8, local copies, waits for them, and re-layouts, weighted_values(): return lax.scan(advance, start_state, (scores, value_blocks))[0]  65.5 us
    all_gather x1, waiting for transfers between devices, body(): gathered = lax.all_gather(normed, 'col', axis=0, tiled=True)  50.2 us
    all_gather x1, waiting for transfers between devices, body(): attention_all = lax.all_gather(attended, 'row', axis=0, tiled=True)  44.1 us
    reduce_scatter x1, waiting for transfers between devices, body(): lax.psum_scatter(jnp.dot(gathered, combined, preferred_element_type=jnp.f...  42.3 us
    reduce_scatter x1, waiting for transfers between devices, body(): lax.psum_scatter(cache_part.reshape(tokens, qwidth).astype(jnp.bfloat16),...  41.3 us
    all_gather x1, waiting for transfers between devices, body(): lax.all_gather(queries.reshape(tok_dev, qwidth), 'row', axis=0, tiled=True)  40.4 us
    dot_general x5, matrix products, advance(): jnp.einsum('htk,kd->thd', weights, block_item[1], preferred_element_type=...  35.5 us
  transfers between devices with their start and end apart: 7, of which 7 were waited for; matrix products, arithmetic and copies ran while one was open for 2% of the time, Pallas kernels for 0%

commit v1 on v0

--- a/solution.py
+++ b/solution.py
@@ -3,6 +3,7 @@
 import jax.numpy as jnp
 from jax import lax
 from jax.sharding import PartitionSpec as P
+from jax.lax import all_to_all, axis_size
 
 D = 8192
 H = 64
@@ -150,9 +151,13 @@
     cache_len = cache_dev * row_count
     cache_head = lax.dynamic_slice_in_dim(cache_keyval, kv_head * HD, HD, 2)
     span_index = cache_len + jnp.arange(tokens, dtype=jnp.int32)
-    all_queries = lax.all_gather(
-        queries.reshape(tok_dev, qwidth), "row", axis=0, tiled=True
-    ).reshape(tokens, heads_dev, HD)
+
+    def lay_the_desk(my_data):
+        return jnp.concatenate(
+            all_to_all(jnp.stack([my_data for _ in range(axis_size("row"))]), "row", 0, 0), axis=0
+        )
+
+    all_queries = lay_the_desk(queries.reshape(tok_dev, qwidth)).reshape(tokens, heads_dev, HD)
     every_index = jnp.arange(tokens, dtype=jnp.int32)
     cache_index = row_index * cache_dev + jnp.arange(cache_dev, dtype=jnp.int32)
     cache_scores = score_blocks(

time: 628 us -> 594 us (0.946)
  waiting for transfers between devices: 332 us -> 281 us
  matrix products: 70.3 us -> 77.1 us
    all_gather x1 -> x0, waiting for transfers between devices: 40.4 us -> none  [body(): lax.all_gather(queries.reshape(tok_dev, qwidth), 'row', axis=0, tiled=True)]
    all_gather x1, waiting for transfers between devices: 31.9 us -> 0.02 us  [body(): lax.all_gather(jnp.concatenate([own_keys, own_values], axis=1), 'row', ax...]
    all_to_all x0 -> x1, waiting for transfers between devices: none -> 20.6 us  [lay_the_desk(): all_to_all(jnp.stack([my_data for _ in range(axis_size('row'))]), 'row',...]
    dot_general x5, matrix products: 21.7 us -> 28.2 us  [block_scores(): jnp.einsum('thd,kd->htk', queries, key_block, preferred_element_type=jnp....]
  transfers between devices with their start and end apart: 7 -> 7, of which waited for: 7 -> 6; matrix products, arithmetic and copies ran while one was open for 2% -> 12% of each run, Pallas kernels for 0% -> 0%
where the time goes in v1:
time: 594 us; the launch traced here: 593 us
  waiting for transfers between devices  281 us (47%)
  local copies, waits for them, and re-layouts  83.7 us (14%)
  blocking collectives  83 us (14%)
  matrix products  77.1 us (13%)
  other arithmetic  49.2 us (8%)
  between operations  14.5 us (2%)
    reduce_scatter x1, waiting for transfers between devices, body(): lax.psum_scatter(jnp.dot(attention_all, out_weight, preferred_element_typ...  81.9 us
    dynamic_slice x8, local copies, waits for them, and re-layouts, weighted_values(): return lax.scan(advance, start_state, (scores, value_blocks))[0]  65.5 us
    all_gather x1, waiting for transfers between devices, body(): gathered = lax.all_gather(normed, 'col', axis=0, tiled=True)  50.2 us
    all_gather x1, waiting for transfers between devices, body(): attention_all = lax.all_gather(attended, 'row', axis=0, tiled=True)  44.3 us
    reduce_scatter x1, waiting for transfers between devices, body(): lax.psum_scatter(jnp.dot(gathered, combined, preferred_element_type=jnp.f...  42.6 us
    reduce_scatter x1, waiting for transfers between devices, body(): lax.psum_scatter(cache_part.reshape(tokens, qwidth).astype(jnp.bfloat16),...  41 us
    dot_general x5, matrix products, advance(): jnp.einsum('htk,kd->thd', weights, block_item[1], preferred_element_type=...  35.5 us
    pmax x1, blocking collectives, body(): lax.pmax(jnp.maximum(cache_peak, placed_peak).astype(jnp.bfloat16), 'row')  32.6 us
  transfers between devices with their start and end apart: 7, of which 6 were waited for; matrix products, arithmetic and copies ran while one was open for 12% of the time, Pallas kernels for 0%

profile of v1, /device:TPU:0, one launch (start us, length us, event | category | flops | bytes accessed | tf_op | source)
XLA Modules:
  0.0 592.6 jit_solution(13343225604243025345)
XLA Ops:
  7.7 19.8 %psum.14 = f32[128]{0:T(128)S(1)} all-reduce(f32[128]{0:T(128)S(1)} %fusion.27), channel_id=1, replica_groups=mesh['row'=8,'col'=16] {'row'}, use_global_device_ids=true, to_apply=%region_1.0 | all-reduce | flops 128 | bytes 1024 | tf_op jit(solution)/shard_map/psum | solution.py:101
  34.3 50.2 %all-gather.4.cloned.1.call-done = bf16[2048,1024]{1,0:T(8,128)(2,1)} async-done(((bf16[128,1024]{1,0:T(8,128)(2,1)}), bf16[2048,1024]{1,0:T(8,128)(2,1)}) %all-gather.4.cloned.1.call-update) | async-done | bytes 4194320 | tf_op jit(solution)/shard_map/all_gather | solution.py:104
  93.0 42.6 %reduce-scatter.4.cloned.1.call-done = bf16[256,768]{0,1:T(8,128)(2,1)} async-done(((bf16[2048,768]{0,1:T(8,128)(2,1)}), bf16[256,768]{0,1:T(8,128)(2,1)}) %reduce-scatter.4.cloned.1.call-update) | async-done | bytes 393232 | tf_op jit(solution)/shard_map/reduce_scatter | solution.py:126
  148.5 20.6 %all-to-all-done = bf16[8,256,512]{1,2,0:T(8,128)(2,1)S(1)} async-done(((bf16[8,256,512]{1,2,0:T(8,128)(2,1)}), bf16[8,256,512]{1,2,0:T(8,128)(2,1)S(1)}, u32[]{:S(2)}, u32[]{:S(2)}) %all-to-all-start) | async-done | bytes 2097184 | tf_op jit(solution)/shard_map/all_to_all | solution.py:157
  178.8 27.7 %while.34 = (s32[]{:T(128)}, f32[4,4,2048,256]{2,3,1,0:T(8,128)}, s32[4,256]{1,0:T(4,128)S(1)}, s32[]{:T(128)}, bf16[4,256,128]{2,1,0:T(8,128)(2,1)}, /*index=5*/bf16[2048,4,128]{2,0,1:T(8,128)(2,1)S(1)}) while((s32[]{:T(128)}, f32[4,4,2048,256]{2,3,1,0:T(8,128)}, s32[4,256]{1,0:T(4,128)S(1)}, s32[]{:T(128)}, ...), condition=%wide.region_4.5_spmd.clone.clone, body=%wide.region_3.4_spmd.clone.sunk.clone | while | flops 542114560 | bytes 11606097 | solution.py:57
  206.5 12.0 %reduce_max.18 = f32[4,2048]{1,0:T(4,128)S(1)} reduce(f32[4,4,2048,256]{2,3,1,0:T(8,128)} %get-tuple-element.426, f32[]{:T(128)} %constant.145.clone.1), dimensions={0,3}, to_apply=%region_5.6 | reduce | flops 8380416 | bytes 33587204 | tf_op jit(solution)/shard_map/reduce_max | solution.py:61
  218.5 14.1 %select_reduce_fusion = f32[4,2048]{1,0:T(4,128)S(1)} fusion(f32[4,4,2048,256]{2,3,1,0:T(8,128)} %get-tuple-element.426, f32[4,2048]{1,0:T(4,128)S(1)} %reduce_max.18), kind=kLoop, calls=%fused_computation.20 | loop fusion | flops 33546240 | bytes 33619968 | tf_op jit(solution)/shard_map/reduce_sum | solution.py:63
  238.4 32.6 %pmax.7 = bf16[4,2048]{1,0:T(4,128)(2,1)S(1)} all-reduce(bf16[4,2048]{1,0:T(4,128)(2,1)S(1)} %max.7), channel_id=1, replica_groups=mesh['row'=8,'col'=16] {'row'}, use_global_device_ids=true, to_apply=%region_7.8 | all-reduce | flops 8192 | bytes 32768 | tf_op jit(solution)/shard_map/pmax | solution.py:175
  275.7 30.6 %psum.15 = bf16[4,2048]{1,0:T(4,128)(2,1)S(1)} all-reduce(bf16[4,2048]{1,0:T(4,128)(2,1)S(1)} %convert_element_type.114), channel_id=1, replica_groups=mesh['row'=8,'col'=16] {'row'}, use_global_device_ids=true, to_apply=%region_10.11 | all-reduce | flops 8192 | bytes 32768 | tf_op jit(solution)/shard_map/psum | solution.py:182
  306.4 95.3 %while.35 = (s32[]{:T(128)}, f32[2048,4,128]{0,2,1:T(8,128)}, bf16[4,256,128]{2,1,0:T(8,128)(2,1)}, f32[4,4,2048,256]{2,3,1,0:T(8,128)}, f32[4,2048]{1,0:T(4,128)S(1)}, /*index=5*/f32[4,2048]{1,0:T(4,128)S(1)}) while((s32[]{:T(128)}, f32[2048,4,128]{0,2,1:T(8,128)}, bf16[4,256,128]{2,1,0:T(8,128)(2,1)}, ...), condition=%wide.region_12.13_spmd.clone.clone, body=%wide.region_11.12_spmd.clone.sunk.clone | while | flops 545259520 | bytes 50463312 | solution.py:80
  306.4 7.7 %constant_dynamic-slice_fusion.8 = f32[1,4,2048,256]{2,3,1,0:T(8,128)} fusion(f32[4,4,2048,256]{2,3,1,0:T(8,128)} %get-tuple-element.438, s32[]{:T(128)} %get-tuple-element.429), kind=kLoop, calls=%fused_computation.7.clone.1.clone | loop fusion | bytes 16777220 | tf_op jit(solution)/shard_map/while/body/jit(dynamic_index_in_dim)/dynamic_slice | solution.py:80
  314.1 8.7 %copy.64 = f32[1,4,2048,256]{3,2,1,0:T(8,128)} copy(f32[1,4,2048,256]{2,3,1,0:T(8,128)} %constant_dynamic-slice_fusion.8) | data formatting | bytes 16777216 | tf_op jit(solution)/shard_map/while/body/jit(dynamic_index_in_dim)/dynamic_slice | solution.py:80
  329.6 7.7 %constant_dynamic-slice_fusion.8 = f32[1,4,2048,256]{2,3,1,0:T(8,128)} fusion(f32[4,4,2048,256]{2,3,1,0:T(8,128)} %get-tuple-element.438, s32[]{:T(128)} %get-tuple-element.429), kind=kLoop, calls=%fused_computation.7.clone.1.clone | loop fusion | bytes 16777220 | tf_op jit(solution)/shard_map/while/body/jit(dynamic_index_in_dim)/dynamic_slice | solution.py:80
  337.2 8.7 %copy.64 = f32[1,4,2048,256]{3,2,1,0:T(8,128)} copy(f32[1,4,2048,256]{2,3,1,0:T(8,128)} %constant_dynamic-slice_fusion.8) | data formatting | bytes 16777216 | tf_op jit(solution)/shard_map/while/body/jit(dynamic_index_in_dim)/dynamic_slice | solution.py:80
  345.9 7.7 %bitcast_add_fusion.3 = f32[2048,4,128]{0,2,1:T(8,128)} fusion(f32[2048,4,128]{0,2,1:T(8,128)} %get-tuple-element.430, f32[4,2048]{1,0:T(4,128)S(1)} %get-tuple-element.440, f32[1,4,2048,256]{3,2,1,0:T(8,128)} %copy.64, f32[4,2048]{1,0:T(4,128)S(1)} %get-tuple-element.439, pred[]{:T(512)S(6)} %compare.8, ...), kind=kOutput, calls=%fused_computation.2.clone.1.clone | convolution fusion | flops 545259520 | bytes 16908800 | tf_op jit(solution)/shard_map/while/body/eval_jaxpr/htk,kd->thd/dot_general | solution.py:75
  353.6 7.7 %constant_dynamic-slice_fusion.8 = f32[1,4,2048,256]{2,3,1,0:T(8,128)} fusion(f32[4,4,2048,256]{2,3,1,0:T(8,128)} %get-tuple-element.438, s32[]{:T(128)} %get-tuple-element.429), kind=kLoop, calls=%fused_computation.7.clone.1.clone | loop fusion | bytes 16777220 | tf_op jit(solution)/shard_map/while/body/jit(dynamic_index_in_dim)/dynamic_slice | solution.py:80
  361.3 8.7 %copy.64 = f32[1,4,2048,256]{3,2,1,0:T(8,128)} copy(f32[1,4,2048,256]{2,3,1,0:T(8,128)} %constant_dynamic-slice_fusion.8) | data formatting | bytes 16777216 | tf_op jit(solution)/shard_map/while/body/jit(dynamic_index_in_dim)/dynamic_slice | solution.py:80
  369.9 7.7 %bitcast_add_fusion.3 = f32[2048,4,128]{0,2,1:T(8,128)} fusion(f32[2048,4,128]{0,2,1:T(8,128)} %get-tuple-element.430, f32[4,2048]{1,0:T(4,128)S(1)} %get-tuple-element.440, f32[1,4,2048,256]{3,2,1,0:T(8,128)} %copy.64, f32[4,2048]{1,0:T(4,128)S(1)} %get-tuple-element.439, pred[]{:T(512)S(6)} %compare.8, ...), kind=kOutput, calls=%fused_computation.2.clone.1.clone | convolution fusion | flops 545259520 | bytes 16908800 | tf_op jit(solution)/shard_map/while/body/eval_jaxpr/htk,kd->thd/dot_general | solution.py:75
  377.6 7.7 %constant_dynamic-slice_fusion.8 = f32[1,4,2048,256]{2,3,1,0:T(8,128)} fusion(f32[4,4,2048,256]{2,3,1,0:T(8,128)} %get-tuple-element.438, s32[]{:T(128)} %get-tuple-element.429), kind=kLoop, calls=%fused_computation.7.clone.1.clone | loop fusion | bytes 16777220 | tf_op jit(solution)/shard_map/while/body/jit(dynamic_index_in_dim)/dynamic_slice | solution.py:80
  385.3 8.7 %copy.64 = f32[1,4,2048,256]{3,2,1,0:T(8,128)} copy(f32[1,4,2048,256]{2,3,1,0:T(8,128)} %constant_dynamic-slice_fusion.8) | data formatting | bytes 16777216 | tf_op jit(solution)/shard_map/while/body/jit(dynamic_index_in_dim)/dynamic_slice | solution.py:80
  394.0 7.7 %bitcast_add_fusion.3 = f32[2048,4,128]{0,2,1:T(8,128)} fusion(f32[2048,4,128]{0,2,1:T(8,128)} %get-tuple-element.430, f32[4,2048]{1,0:T(4,128)S(1)} %get-tuple-element.440, f32[1,4,2048,256]{3,2,1,0:T(8,128)} %copy.64, f32[4,2048]{1,0:T(4,128)S(1)} %get-tuple-element.439, pred[]{:T(512)S(6)} %compare.8, ...), kind=kOutput, calls=%fused_computation.2.clone.1.clone | convolution fusion | flops 545259520 | bytes 16908800 | tf_op jit(solution)/shard_map/while/body/eval_jaxpr/htk,kd->thd/dot_general | solution.py:75
  405.9 41.0 %reduce-scatter.6.cloned.1.call-done = bf16[256,512]{0,1:T(8,128)(2,1)} async-done(((bf16[2048,512]{0,1:T(8,128)(2,1)}), bf16[256,512]{0,1:T(8,128)(2,1)}) %reduce-scatter.6.cloned.1.call-update) | async-done | bytes 262160 | tf_op jit(solution)/shard_map/reduce_scatter | solution.py:187
  452.6 44.3 %all-gather.8.cloned.1.call-done = bf16[2048,512]{0,1:T(8,128)(2,1)} async-done(((bf16[256,512]{0,1:T(8,128)(2,1)}), bf16[2048,512]{0,1:T(8,128)(2,1)}) %all-gather.8.cloned.1.call-update) | async-done | bytes 2097168 | tf_op jit(solution)/shard_map/all_gather | solution.py:196
  503.8 81.9 %reduce-scatter.8.cloned.1.call-done = bf16[128,1024]{1,0:T(8,128)(2,1)} async-done(((bf16[2048,1024]{1,0:T(8,128)(2,1)}), bf16[128,1024]{1,0:T(8,128)(2,1)}) %reduce-scatter.8.cloned.1.call-update) | async-done | bytes 262160 | tf_op jit(solution)/shard_map/reduce_scatter | solution.py:198
  (97 shorter events, 99.8 us)
Async XLA Ops:
  6.5 27.4 %copy-start.2 = (bf16[1024,512]{1,0:T(8,128)(2,1)S(1)}, bf16[1024,512]{1,0:T(8,128)(2,1)}, u32[]{:S(2)}) copy-start(bf16[1024,512]{1,0:T(8,128)(2,1)} %param.18) | copy-start | bytes 3145732
  6.5 78.0 %all-gather.4.cloned.1.call-start = ((), (), s32[]{:S(2)}) async-start(), calls=%async_computation.4 | async-start | bytes 4456448 | tf_op jit(solution)/shard_map/all_gather | solution.py:104
  29.3 106.3 %reduce-scatter.4.cloned.1.call-start = ((), (), s32[]{:S(2)}) async-start(), calls=%async_computation.5 | async-start | bytes 3538944 | tf_op jit(solution)/shard_map/reduce_scatter | solution.py:126
  91.8 44.9 %copy-start.4 = (f32[512]{0:T(512)S(1)}, f32[512]{0:T(512)}, u32[]{:S(2)}) copy-start(f32[512]{0:T(512)} %param.20) | copy-start | bytes 6148
  137.6 1.6 copy-start
  139.3 29.8 %all-to-all-start = ((bf16[8,256,512]{1,2,0:T(8,128)(2,1)}), bf16[8,256,512]{1,2,0:T(8,128)(2,1)S(1)}, u32[]{:S(2)}, u32[]{:S(2)}) async-start(bf16[8,256,512]{1,2,0:T(8,128)(2,1)} %stack.3), calls=%async_computation.1 | async-start | bytes 4194304 | tf_op jit(solution)/shard_map/all_to_all | solution.py:157
  142.9 89.7 %all-gather.6.cloned.1.call-start = ((), (), s32[]{:S(2)}) async-start(), calls=%async_computation.6 | async-start | bytes 1179648 | tf_op jit(solution)/shard_map/all_gather | solution.py:145
  148.2 298.6 %reduce-scatter.6.cloned.1.call-start = ((), (), s32[]{:S(2)}) async-start(), calls=%async_computation.7 | async-start | bytes 2359296 | tf_op jit(solution)/shard_map/reduce_scatter | solution.py:187
  218.5 14.1 %copy-start.1 = (bf16[256,4,128]{2,0,1:T(8,128)(2,1)S(1)}, bf16[256,4,128]{2,0,1:T(8,128)(2,1)}, u32[]{:S(2)}) copy-start(bf16[256,4,128]{2,0,1:T(8,128)(2,1)} %copy-done) | copy-start | bytes 786436
  401.7 45.2 %copy-start.3 = (bf16[2048,256]{0,1:T(8,128)(2,1)S(1)}, bf16[2048,256]{0,1:T(8,128)(2,1)}, u32[]{:S(2)}) copy-start(bf16[2048,256]{0,1:T(8,128)(2,1)} %all-gather.6.cloned.1.call-done) | copy-start | bytes 3145732
  405.6 91.3 %all-gather.8.cloned.1.call-start = ((), (), s32[]{:S(2)}) async-start(), calls=%async_computation.8 | async-start | bytes 2359296 | tf_op jit(solution)/shard_map/all_gather | solution.py:196
  446.9 50.0 %copy-start.5 = (f32[4,8]{1,0:T(4,128)S(1)}, f32[4,8]{1,0:T(4,128)}, u32[]{:S(2)}) copy-start(f32[4,8]{1,0:T(4,128)} %param.25) | copy-start | bytes 388
  452.5 133.2 %reduce-scatter.8.cloned.1.call-start = ((), (), s32[]{:S(2)}) async-start(), calls=%async_computation.9 | async-start | bytes 4456448 | tf_op jit(solution)/shard_map/reduce_scatter | solution.py:198
Sparse Core Ops, SparseCore 0:
  29.5 55.0 all-gather.3
  91.9 43.6 reduce-scatter.3
  148.4 41.5 all-gather.5
  405.7 41.0 reduce-scatter.5
  452.7 44.1 all-gather.7
  503.9 81.7 reduce-scatter.7
